TPU v7x, 32 devices: a whole 2x2x4 slice. The times are simulated.
32 devices in a mesh: space: 8 (over z, x), chan: 4 (over y, core).
Axes of the slice: x: 2, y: 2, z: 4, core: 2. Of those that a mesh axis runs over, the one named last changes fastest.
Arguments:
- features: float32 [256, 4096], P('chan', 'space'), may hold values from -6 to 6
- positions: float32 [3, 4096], P(None, 'space'), may hold values from 0 to 2, as said below
- counts: int32 [16], P('space'), may hold values from 1 to 256, as said below
- neighbours: int32 [16, 4], P('space'), may hold values from 0 to 5, as said below
- wavevectors: int32 [3, 512], replicated, may hold values from -4 to 4, as said below
- filters: float32 [8, 256, 256], P(None, 'chan'), may hold values from -0.125 to 0.125
- cotangent: float32 [256, 4096], P('chan', 'space'), may hold values from -6 to 6
Outputs:
- updated: float32 [256, 4096], P('chan', 'space')
- grad_features: float32 [256, 4096], P('chan', 'space')
Inputs may be any that keep to these rules, and one draw needn't show every extreme that they name: `counts`: at least one block holds 256 live atoms. `neighbours`: entry e names block e mod 2 of the previous (e // 2 = 0), the same (1) or the next (2) slab layer, the layers closing into a loop; the first entry of a row is the block itself, the entries of a row differ, and each names a block whose position within its layer differs from the row's by at most one. `wavevectors`: no column is all zeros. `positions`: the first coordinate lies in [0, 1], the second in [b, b + 1] for the b-th block of a layer, the third in [0, 1].
All inputs are finite; a program needn't handle non-finite values.
Results may differ from a plain program's by a relative error of at most 0.0003.
Values sent between devices are 32-bit elements; how exact they have to be, the bound alone decides.
A program may use at most 64 MiB of HBM per device.

v0:
```python
import functools
import math

import jax
import jax.numpy as jnp
from jax import lax
from jax.experimental import pallas as pl
from jax.experimental.pallas import tpu as pltpu
from jax.sharding import PartitionSpec as P

NRAD = 8
NB = 4
BLK_DEV = 2
MOST = 4
SIDE = 2 * MOST + 1
HALF = (SIDE**3 - 1) // 2
MESH = pl.DeviceIdType.MESH
f32 = jnp.float32
bf16 = jnp.bfloat16


def halves(x):
    high = x.astype(bf16)
    return high, (x - high.astype(f32)).astype(bf16)


def dot(a, b):
    return jnp.dot(a, b, preferred_element_type=f32)


def dot_nt(a, b):
    return lax.dot_general(a, b, (((1,), (1,)), ((), ())), preferred_element_type=f32)


def turn_cos_sin(p):
    r = (p - jnp.floor(p + 0.5)) * math.pi
    s2 = r * r
    s = 1.0 / 6227020800.0
    for n in (-1.0 / 39916800.0, 1.0 / 362880.0, -1.0 / 5040.0, 1.0 / 120.0, -1.0 / 6.0, 1.0):
        s = s * s2 + n
    s = s * r
    c = 1.0 / 479001600.0
    for n in (-1.0 / 3628800.0, 1.0 / 40320.0, -1.0 / 720.0, 1.0 / 24.0, -0.5, 1.0):
        c = c * s2 + n
    return 1.0 - 2.0 * s * s, 2.0 * s * c


def lattice(first, rows):
    f = lax.broadcasted_iota(jnp.int32, (rows, 1), 0).astype(f32) + (first + HALF + 1.0)
    a = jnp.floor((f + 0.5) * (1.0 / (SIDE * SIDE)))
    rest = f - a * (SIDE * SIDE)
    b = jnp.floor((rest + 0.5) * (1.0 / SIDE))
    c = rest - b * SIDE
    return f, a - MOST, b - MOST, c - MOST


def kernel(n, chans, feat, pos, counts, nbr, wv, filt, cot, upd, grad,
           f6, p6, pt, fx, cm, c2, gh, gl, mt, mts, th, tl, ss, rb, sg, ps, rx, ug, so, sr,
           re, wo, wp, rw, rt, hb, misc_s, misc_r, red_s, red_r, gat_s, gat_r):
    panel, slots = feat.shape
    cap = slots // BLK_DEV
    rows_all = th.shape[0]
    lat = rows_all // 2
    piece = ss.shape[1]
    pair = 2 * panel
    groups = chans // 2
    s = lax.axis_index("space")
    q = lax.axis_index("chan")
    p = lax.rem(q, 2)
    h = lax.div(q, 2)
    mate = (s, q + 1 - 2 * p)
    nxt = (lax.rem(s + 1, n), q)
    prv = (lax.rem(s + n - 1, n), q)

    def remote(src, dst, at, dev):
        return pltpu.make_async_remote_copy(
            src_ref=src, dst_ref=dst, send_sem=misc_s.at[at], recv_sem=misc_r.at[at],
            device_id=dev, device_id_type=MESH)

    lane = lax.broadcasted_iota(jnp.int32, (1, slots), 1)
    bound = jnp.where(lane < cap, counts[0], counts[1] + cap)
    live = (lane < bound).astype(f32)
    fm = feat[...] * live
    cmask = cot[...] * live
    f6[1, 0] = fm
    for b in range(BLK_DEV):
        cm[b] = cmask[:, b * cap:(b + 1) * cap]
    p6[1] = jnp.zeros(p6.shape[1:], f32)
    for b in range(BLK_DEV):
        p6[1, b, 0:3, :] = pos[:, b * cap:(b + 1) * cap]

    barrier = pltpu.get_barrier_semaphore()

    def greet(k, carry):
        pl.semaphore_signal(barrier, inc=1, device_id=(lax.rem(s + k, n), q), device_id_type=MESH)
        return carry

    lax.fori_loop(1, n, greet, 0)
    pl.semaphore_signal(barrier, inc=1, device_id=mate, device_id_type=MESH)
    for k in range(1, groups):
        pl.semaphore_signal(barrier, inc=1, device_id=(s, lax.rem(q + 2 * k, chans)), device_id_type=MESH)
    pl.semaphore_wait(barrier, n - 1 + 1 + groups - 1)

    pos_up = remote(p6.at[1], p6.at[0], 0, nxt)
    pos_dn = remote(p6.at[1], p6.at[2], 1, prv)
    feat_up = remote(f6.at[1, 0], f6.at[0, 0], 2, nxt)
    feat_dn = remote(f6.at[1, 0], f6.at[2, 0], 3, prv)
    feat_mate = remote(f6.at[1, 0], f6.at[1, 1], 4, mate)
    fwd_lo = remote(f6.at[0, 0], f6.at[0, 1], 5, mate)
    fwd_hi = remote(f6.at[2, 0], f6.at[2, 1], 6, mate)
    filt_mate = remote(filt, fx, 7, mate)
    cot_mate = remote(cm.at[1 - p], c2.at[p], 8, mate)
    for c in (pos_up, pos_dn, feat_up, feat_dn, feat_mate, filt_mate, cot_mate):
        c.start()
    c2[p] = cm[p]

    chunk = 16
    layer_x = s.astype(f32)
    xs = (pos[0:1, :] + layer_x) * (1.0 / n)
    ys = pos[1:2, :] * (1.0 / BLK_DEV)
    zs = pos[2:3, :]

    def table(i, carry):
        at = pl.multiple_of(i * chunk, chunk)
        _, a, b, c = lattice((i * chunk).astype(f32), chunk)
        cosv, sinv = turn_cos_sin(a * xs + b * ys + c * zs)
        ch, cl = halves(cosv)
        sh, sl = halves(sinv)
        th[pl.ds(at, chunk), :] = ch
        tl[pl.ds(at, chunk), :] = cl
        th[pl.ds(lat + at, chunk), :] = sh
        tl[pl.ds(lat + at, chunk), :] = sl
        return carry

    lax.fori_loop(0, lat // chunk, table, 0)
    vh, vl = halves(jnp.concatenate([fm, cmask], 0))
    two = dot_nt(th[...], jnp.concatenate([vh, vl], 0))
    full = two[:, :pair] + two[:, pair:] + dot_nt(tl[...], vh)
    ss[...] = full.reshape(n, piece, pair)

    def reduce_copy(k):
        return pltpu.make_async_remote_copy(
            src_ref=ss.at[lax.rem(s + k, n)], dst_ref=rb.at[s], send_sem=red_s.at[k],
            recv_sem=red_r.at[k], device_id=(lax.rem(s + k, n), q), device_id_type=MESH)

    def start_reduce(k, carry):
        reduce_copy(k).start()
        return carry

    feat_up.wait_recv()
    fwd_lo.start()
    feat_dn.wait_recv()
    fwd_hi.start()
    lax.fori_loop(1, n, start_reduce, 0)

    pos_up.wait_recv()
    pos_dn.wait_recv()
    pt[...] = p6[1, p].T
    step = 16
    chosen = [nbr[p, e] for e in range(NB)]

    def radial(i, carry):
        at = pl.multiple_of(i * step, step)
        own = pt[pl.ds(at, step), :]
        for e in range(NB):
            w = chosen[e]
            far = p6[lax.div(w, BLK_DEV), lax.rem(w, BLK_DEV)]
            offset = (lax.div(w, BLK_DEV) - 1).astype(f32)
            dx = own[:, 0:1] - (far[0:1, :] + offset)
            dy = own[:, 1:2] - far[1:2, :]
            dz = own[:, 2:3] - far[2:3, :]
            sq = jnp.minimum(dx * dx + dy * dy + dz * dz, 1.0)
            left = 1.0 - sq
            u = NRAD * jnp.sqrt(sq) - 0.5
            t = jnp.exp(u)
            g = jnp.exp(-0.5 * u * u) * (0.3 * left * left)
            for r in range(NRAD):
                if r:
                    g = g * (t * math.exp(0.5 - r))
                a, b = halves(g)
                gh[r, pl.ds(at, step), e * cap:(e + 1) * cap] = a
                gl[r, pl.ds(at, step), e * cap:(e + 1) * cap] = b
        return carry

    lax.fori_loop(0, cap // step, radial, 0)

    feat_mate.wait_recv()
    fwd_lo.wait_recv()
    fwd_hi.wait_recv()
    for layer in range(3):
        both = jnp.concatenate([f6[layer, 0], f6[layer, 1]], 0)
        for b in range(BLK_DEV):
            a, c = halves(both[:, b * cap:(b + 1) * cap].T)
            mt[layer * BLK_DEV + b] = jnp.concatenate([a, c], 1)
    for e in range(NB):
        mts[e * cap:(e + 1) * cap, :] = mt[chosen[e]]
    filt_mate.wait_recv()

    def filters_of(r):
        return halves(jnp.concatenate([filt[r], fx[r]], 0))

    def forward(r, total):
        two = dot(gh[r], mts[...])
        sums = two[:, :pair] + two[:, pair:] + dot(gl[r], mts[:, :pair])
        a, b = halves(sums)
        fh, fl = filters_of(r)
        return total + dot(jnp.concatenate([a, b], 1), jnp.concatenate([fh, fh], 0)) + dot(a, fl)

    total = lax.fori_loop(0, NRAD, forward, jnp.zeros((cap, groups * pair), f32))
    for k in range(groups):
        ps[k] = total[:, k * pair:(k + 1) * pair]
    pre_copies = []
    for k in range(1, groups):
        c = remote(ps.at[lax.rem(h + k, groups)], rx.at[k - 1], 16 + k, (s, lax.rem(q + 2 * k, chans)))
        c.start()
        pre_copies.append(c)

    def wait_reduce(k, carry):
        reduce_copy(k).wait_recv()
        return carry

    lax.fori_loop(1, n, wait_reduce, 0)
    rb[s] = ss[s]

    def add_up(k, acc):
        return acc + rb[k]

    sg[s] = lax.fori_loop(0, n, add_up, jnp.zeros((piece, pair), f32))

    def gather_copy(k):
        return pltpu.make_async_remote_copy(
            src_ref=sg.at[s], dst_ref=sg.at[s], send_sem=gat_s.at[k],
            recv_sem=gat_r.at[k], device_id=(lax.rem(s + k, n), q), device_id_type=MESH)

    def start_gather(k, carry):
        gather_copy(k).start()
        return carry

    lax.fori_loop(1, n, start_gather, 0)

    for c in pre_copies:
        c.wait_recv()
    acc = ps[h]
    for k in range(1, groups):
        acc = acc + rx[k - 1]
    pre = acc.T
    cot_mate.wait_recv()
    sigma = 1.0 / (1.0 + jnp.exp(-pre))
    act = pre * sigma
    ug[h] = jnp.concatenate([c2[0], c2[1]], 0) * sigma * (1.0 + pre * (1.0 - sigma))
    up_copies = []
    for k in range(1, groups):
        c = pltpu.make_async_remote_copy(
            src_ref=ug.at[h], dst_ref=ug.at[h], send_sem=misc_s.at[24 + k], recv_sem=misc_r.at[24 + k],
            device_id=(s, lax.rem(q + 2 * k, chans)), device_id_type=MESH)
        c.start()
        up_copies.append(c)
    so[0] = act[:panel]
    so[1] = act[panel:]
    act_mate = remote(so.at[1 - p], sr, 9, mate)
    act_mate.start()

    f, a, b, c = lattice(0.0, lat)
    wf = wv[...].astype(f32) + MOST
    key = (wf[0:1] * SIDE + wf[1:2]) * SIDE + wf[2:3]
    hit = (key == f).astype(f32) + ((2.0 * HALF - key) == f).astype(f32)
    times = jnp.sum(hit, axis=1, keepdims=True)
    qa = a * (2.0 * math.pi / n)
    qb = b * (2.0 * math.pi / BLK_DEV)
    qc = c * (2.0 * math.pi)
    k2 = qa * qa + qb * qb + qc * qc
    raw = jnp.exp(-k2 / 2000.0) / (k2 + 100.0)
    norm = jnp.sum(times * raw * raw, axis=0, keepdims=True)
    weight = times * raw * lax.rsqrt(norm) * math.sqrt(3.0 / (n * slots))
    weight = jnp.concatenate([weight, weight], 0)

    def wait_gather(k, carry):
        gather_copy(k).wait_recv()
        return carry

    lax.fori_loop(1, n, wait_gather, 0)
    sh, sl = halves((sg[...].reshape(rows_all, pair) * weight).T)
    two = dot(jnp.concatenate([sh, sl], 0), th[...])
    far_part = two[:pair] + two[pair:] + dot(sh, tl[...])

    for c in up_copies:
        c.wait_recv()
    uh, ul = halves(ug[...].reshape(groups * pair, cap))
    re[...] = jnp.zeros(re.shape, f32)

    def backward(r, carry):
        fh, fl = filters_of(r)
        two = dot(jnp.concatenate([fh, fl], 0), uh)
        a, b = halves(two[:pair] + two[pair:] + dot(fh, ul))
        out = dot(jnp.concatenate([a, b], 0), gh[r])
        re[...] += out[:pair] + out[pair:] + dot(a, gl[r])
        return carry

    lax.fori_loop(0, NRAD, backward, 0)
    for w in range(3 * BLK_DEV):
        acc = jnp.zeros((pair, cap), f32)
        for e in range(NB):
            acc = acc + jnp.where(chosen[e] == w, re[:, e * cap:(e + 1) * cap], 0.0)
        wo[w] = acc[:panel]
        wp[w] = acc[panel:]
    ret_mate = remote(wp, rw, 10, mate)
    ret_mate.start()

    act_mate.wait_recv()
    mine, other = so[p], sr[...]
    first = jnp.where(p == 0, mine, other)
    second = jnp.where(p == 0, other, mine)
    upd[...] = live * (fm + jnp.concatenate([first, second], 1) + far_part[:panel])

    ret_mate.wait_recv()
    for w in range(3 * BLK_DEV):
        rt[w // BLK_DEV, w % BLK_DEV] = wo[w] + rw[w]
    ret_up = remote(rt.at[2], hb.at[0], 11, nxt)
    ret_dn = remote(rt.at[0], hb.at[1], 12, prv)
    ret_up.start()
    ret_dn.start()
    part = cmask + far_part[panel:]
    ret_up.wait_recv()
    ret_dn.wait_recv()
    near = [rt[1, b] + hb[0, b] + hb[1, b] for b in range(BLK_DEV)]
    grad[...] = live * (part + jnp.concatenate(near, 1))

    for c in (pos_up, pos_dn, feat_up, feat_dn, feat_mate, fwd_lo, fwd_hi, filt_mate, cot_mate,
              act_mate, ret_mate, ret_up, ret_dn, *pre_copies, *up_copies):
        c.wait_send()

    def drain(k, carry):
        reduce_copy(k).wait_send()
        gather_copy(k).wait_send()
        return carry

    lax.fori_loop(1, n, drain, 0)


def shards(n, chans, features, positions, counts, neighbours, wavevectors, filters, cotangent):
    panel, slots = features.shape
    cap = slots // BLK_DEV
    pair = 2 * panel
    groups = chans // 2
    piece = -(-(-(-2 * HALF // n)) // 8) * 8
    while (n * piece) % 32:
        piece += 8
    rows = n * piece
    vm = pltpu.VMEM
    scratch = [
        vm((3, 2, panel, slots), f32),
        vm((3, BLK_DEV, 8, cap), f32),
        vm((cap, 8), f32),
        vm(filters.shape, f32),
        vm((BLK_DEV, panel, cap), f32),
        vm((2, panel, cap), f32),
        vm((NRAD, cap, NB * cap), bf16),
        vm((NRAD, cap, NB * cap), bf16),
        vm((3 * BLK_DEV, cap, 2 * pair), bf16),
        vm((NB * cap, 2 * pair), bf16),
        vm((rows, slots), bf16),
        vm((rows, slots), bf16),
        vm((n, piece, pair), f32),
        vm((n, piece, pair), f32),
        vm((n, piece, pair), f32),
        vm((groups, cap, pair), f32),
        vm((max(groups - 1, 1), cap, pair), f32),
        vm((groups, pair, cap), f32),
        vm((2, panel, cap), f32),
        vm((panel, cap), f32),
        vm((pair, NB * cap), f32),
        vm((3 * BLK_DEV, panel, cap), f32),
        vm((3 * BLK_DEV, panel, cap), f32),
        vm((3 * BLK_DEV, panel, cap), f32),
        vm((3, BLK_DEV, panel, cap), f32),
        vm((2, BLK_DEV, panel, cap), f32),
        pltpu.SemaphoreType.DMA((32,)),
        pltpu.SemaphoreType.DMA((32,)),
        pltpu.SemaphoreType.DMA((n,)),
        pltpu.SemaphoreType.DMA((n,)),
        pltpu.SemaphoreType.DMA((n,)),
        pltpu.SemaphoreType.DMA((n,)),
    ]
    whole = pl.BlockSpec(memory_space=pltpu.VMEM)
    small = pl.BlockSpec(memory_space=pltpu.SMEM)
    out = jax.ShapeDtypeStruct((panel, slots), f32)
    return pl.pallas_call(
        functools.partial(kernel, n, chans),
        out_shape=(out, out),
        in_specs=[whole, whole, small, small, whole, whole, whole],
        out_specs=(whole, whole),
        scratch_shapes=scratch,
        compiler_params=pltpu.CompilerParams(
            collective_id=0, has_side_effects=True, vmem_limit_bytes=48 * 1024 * 1024),
    )(features, positions, counts, neighbours, wavevectors, filters, cotangent)


def solution(mesh):
    return jax.shard_map(
        functools.partial(shards, mesh.shape["space"], mesh.shape["chan"]),
        mesh=mesh,
        in_specs=(
            P("chan", "space"),
            P(None, "space"),
            P("space"),
            P("space", None),
            P(),
            P(None, "chan", None),
            P("chan", "space"),
        ),
        out_specs=(P("chan", "space"), P("chan", "space")),
        check_vma=False,
    )
```

profile of v0, /device:TPU:0, one launch (start us, length us, event | category | flops | bytes accessed | tf_op | source)
XLA Modules:
  0.0 54.7 jit_solution(13462154338771549969)
XLA Ops:
  0.6 0.0 copy-start
  0.6 1.0 %copy-done = f32[8,64,256]{2,1,0:T(8,128)S(1)} copy-done((f32[8,64,256]{2,1,0:T(8,128)S(1)}, f32[8,64,256]{2,1,0:T(8,128)}, u32[]{:S(2)}) %copy-start) | copy-done | bytes 524312
  1.7 0.0 copy-start.1
  1.7 0.9 %copy-done.1 = f32[64,512]{1,0:T(8,128)S(1)} copy-done((f32[64,512]{1,0:T(8,128)S(1)}, f32[64,512]{1,0:T(8,128)}, u32[]{:S(2)}) %copy-start.1) | copy-done | bytes 131096
  2.6 0.0 copy-start.2
  2.6 0.9 %copy-done.2 = f32[64,512]{1,0:T(8,128)S(1)} copy-done((f32[64,512]{1,0:T(8,128)S(1)}, f32[64,512]{1,0:T(8,128)}, u32[]{:S(2)}) %copy-start.2) | copy-done | bytes 131096
  3.5 0.0 copy-start.3
  3.5 0.7 %copy-done.3 = f32[3,512]{1,0:T(4,128)S(1)} copy-done((f32[3,512]{1,0:T(4,128)S(1)}, f32[3,512]{1,0:T(4,128)}, u32[]{:S(2)}) %copy-start.3) | copy-done | bytes 6168
  4.2 0.0 copy-start.4
  4.2 0.7 %copy-done.4 = s32[3,512]{1,0:T(4,128)S(1)} copy-done((s32[3,512]{1,0:T(4,128)S(1)}, s32[3,512]{1,0:T(4,128)}, u32[]{:S(2)}) %copy-start.4) | copy-done | bytes 6168
  4.9 0.0 copy-start.5
  4.9 0.7 %copy-done.5 = s32[2,4]{1,0:T(2,128)S(1)} copy-done((s32[2,4]{1,0:T(2,128)S(1)}, s32[2,4]{1,0:T(2,128)}, u32[]{:S(2)}) %copy-start.5) | copy-done | bytes 56
  5.6 0.0 copy-start.6
  5.6 0.7 %copy-done.6 = s32[2]{0:T(128)S(1)} copy-done((s32[2]{0:T(128)S(1)}, s32[2]{0:T(128)}, u32[]{:S(2)}) %copy-start.6) | copy-done | bytes 32
  6.2 47.2 %shard_map.86 = (f32[64,512]{1,0:T(8,128)S(1)}, f32[64,512]{1,0:T(8,128)S(1)}) custom-call(f32[64,512]{1,0:T(8,128)S(1)} %copy-done.1, f32[3,512]{1,0:T(4,128)S(1)} %copy-done.3, s32[2]{0:T(128)S(1)} %copy-done.6, s32[2,4]{1,0:T(2,128)S(1)} %copy-done.5, s32[3,512]{1,0:T(4,128)S(1)} %copy-done.4, f32[8,64,256]{2,1,0:T(8,128)S(1)} %copy-done, ...), custom_call_target="tpu_custom_call" | custom-call | tf_op jit(solution)/shard_map/pallas_call | solution.py:387
  53.4 0.7 %copy.11 = f32[64,512]{1,0:T(8,128)} copy(f32[64,512]{1,0:T(8,128)S(1)} %get-tuple-element.4) | data formatting | bytes 262144
  54.0 0.7 %copy.12 = f32[64,512]{1,0:T(8,128)} copy(f32[64,512]{1,0:T(8,128)S(1)} %get-tuple-element.5) | data formatting | bytes 262144
Async XLA Ops:
  0.6 1.0 %copy-start = (f32[8,64,256]{2,1,0:T(8,128)S(1)}, f32[8,64,256]{2,1,0:T(8,128)}, u32[]{:S(2)}) copy-start(f32[8,64,256]{2,1,0:T(8,128)} %filt.1) | copy-start | bytes 1572868
  1.7 0.9 %copy-start.1 = (f32[64,512]{1,0:T(8,128)S(1)}, f32[64,512]{1,0:T(8,128)}, u32[]{:S(2)}) copy-start(f32[64,512]{1,0:T(8,128)} %feat.1) | copy-start | bytes 393220
  2.6 0.9 %copy-start.2 = (f32[64,512]{1,0:T(8,128)S(1)}, f32[64,512]{1,0:T(8,128)}, u32[]{:S(2)}) copy-start(f32[64,512]{1,0:T(8,128)} %cot.1) | copy-start | bytes 393220
  3.5 0.7 %copy-start.3 = (f32[3,512]{1,0:T(4,128)S(1)}, f32[3,512]{1,0:T(4,128)}, u32[]{:S(2)}) copy-start(f32[3,512]{1,0:T(4,128)} %pos.1) | copy-start | bytes 18436
  4.2 0.7 %copy-start.4 = (s32[3,512]{1,0:T(4,128)S(1)}, s32[3,512]{1,0:T(4,128)}, u32[]{:S(2)}) copy-start(s32[3,512]{1,0:T(4,128)} %wv.1) | copy-start | bytes 18436
  4.9 0.7 %copy-start.5 = (s32[2,4]{1,0:T(2,128)S(1)}, s32[2,4]{1,0:T(2,128)}, u32[]{:S(2)}) copy-start(s32[2,4]{1,0:T(2,128)} %nbr.1) | copy-start | bytes 100
  5.6 0.7 %copy-start.6 = (s32[2]{0:T(128)S(1)}, s32[2]{0:T(128)}, u32[]{:S(2)}) copy-start(s32[2]{0:T(128)} %counts.1) | copy-start | bytes 28
where the time goes:
time: 55 us; the launch traced here: 54.7 us
  Pallas kernels  47.2 us (86%)
  local copies, waits for them, and re-layouts  6.88 us (13%)
  between operations  0.66 us (1%)
    pallas_call x1, Pallas kernels, shards(): pl.pallas_call(functools.partial(kernel, n, chans), out_shape=(out, out),...  47.2 us
    unnamed x16, local copies, waits for them, and re-layouts  6.88 us

commit v1 on v0

v1 whole, which is shorter than its diff:
```python
import functools
import math

import jax
import jax.numpy as jnp
from jax import lax
from jax.experimental import pallas as pl
from jax.experimental.pallas import tpu as pltpu
from jax.sharding import PartitionSpec as P

NRAD = 8
NB = 4
BLK_DEV = 2
PARTS = 2
MOST = 4
SIDE = 2 * MOST + 1
HALF = (SIDE**3 - 1) // 2
MESH = pl.DeviceIdType.MESH
f32 = jnp.float32
bf16 = jnp.bfloat16


def halves(x):
    high = x.astype(bf16)
    return high, (x - high.astype(f32)).astype(bf16)


def dot(a, b):
    return jnp.dot(a, b, preferred_element_type=f32)


def dot_nt(a, b):
    return lax.dot_general(a, b, (((1,), (1,)), ((), ())), preferred_element_type=f32)


def turn_cos_sin(p):
    r = (p - jnp.floor(p + 0.5)) * math.pi
    s2 = r * r
    s = 1.0 / 6227020800.0
    for n in (-1.0 / 39916800.0, 1.0 / 362880.0, -1.0 / 5040.0, 1.0 / 120.0, -1.0 / 6.0, 1.0):
        s = s * s2 + n
    s = s * r
    c = 1.0 / 479001600.0
    for n in (-1.0 / 3628800.0, 1.0 / 40320.0, -1.0 / 720.0, 1.0 / 24.0, -0.5, 1.0):
        c = c * s2 + n
    return 1.0 - 2.0 * s * s, 2.0 * s * c


def lattice(first, rows):
    f = lax.broadcasted_iota(jnp.int32, (rows, 1), 0).astype(f32) + (first + HALF + 1.0)
    a = jnp.floor((f + 0.5) * (1.0 / (SIDE * SIDE)))
    rest = f - a * (SIDE * SIDE)
    b = jnp.floor((rest + 0.5) * (1.0 / SIDE))
    c = rest - b * SIDE
    return f, a - MOST, b - MOST, c - MOST


def kernel(n, chans, feat_in, pos_in, counts_in, nbr_in, wv_in, filt_in, cot_in, upd, grad,
           feat, pos, counts, nbr, wv, filt, cot,
           f6, p6, pt, fx, fh, fl, cm, c2, gh, gl, mts, mt, th, tl, ss, rb, sg, ps, rx, ug, so, sr,
           re, wo, wp, rw, rt, hb, load_s, misc_s, misc_r, red_s, red_r, gat_s, gat_r):
    loads = [
        pltpu.make_async_copy(a, b, load_s.at[i])
        for i, (a, b) in enumerate(zip(
            (feat_in, pos_in, counts_in, nbr_in, wv_in, filt_in, cot_in),
            (feat, pos, counts, nbr, wv, filt, cot)))
    ]
    for c in loads:
        c.start()
    panel, slots = feat.shape
    cap = slots // BLK_DEV
    rows_all = th.shape[0]
    lat = rows_all // 2
    piece = ss.shape[1]
    pair = 2 * panel
    groups = chans // 2
    s = lax.axis_index("space")
    q = lax.axis_index("chan")
    p = lax.rem(q, 2)
    h = lax.div(q, 2)
    mate = (s, q + 1 - 2 * p)
    nxt = (lax.rem(s + 1, n), q)
    prv = (lax.rem(s + n - 1, n), q)

    def remote(src, dst, at, dev):
        return pltpu.make_async_remote_copy(
            src_ref=src, dst_ref=dst, send_sem=misc_s.at[at], recv_sem=misc_r.at[at],
            device_id=dev, device_id_type=MESH)

    barrier = pltpu.get_barrier_semaphore()

    def greet(k, carry):
        pl.semaphore_signal(barrier, inc=1, device_id=(lax.rem(s + k, n), q), device_id_type=MESH)
        return carry

    lax.fori_loop(1, n, greet, 0)
    pl.semaphore_signal(barrier, inc=1, device_id=mate, device_id_type=MESH)
    for k in range(1, groups):
        pl.semaphore_signal(barrier, inc=1, device_id=(s, lax.rem(q + 2 * k, chans)), device_id_type=MESH)

    for at in (0, 1, 2, 6):
        loads[at].wait()
    lane = lax.broadcasted_iota(jnp.int32, (1, slots), 1)
    bound = jnp.where(lane < cap, counts[0], counts[1] + cap)
    live = (lane < bound).astype(f32)
    fm = feat[...] * live
    cmask = cot[...] * live
    f6[1, 0] = fm
    for b in range(BLK_DEV):
        cm[b] = cmask[:, b * cap:(b + 1) * cap]
    p6[1] = jnp.zeros(p6.shape[1:], f32)
    for b in range(BLK_DEV):
        p6[1, b, 0:3, :] = pos[:, b * cap:(b + 1) * cap]

    pl.semaphore_wait(barrier, n - 1 + 1 + groups - 1)

    pos_up = remote(p6.at[1], p6.at[0], 0, nxt)
    pos_dn = remote(p6.at[1], p6.at[2], 1, prv)
    feat_up = remote(f6.at[1, 0], f6.at[0, 0], 2, nxt)
    feat_dn = remote(f6.at[1, 0], f6.at[2, 0], 3, prv)
    feat_mate = remote(f6.at[1, 0], f6.at[1, 1], 4, mate)
    fwd_lo = remote(f6.at[0, 0], f6.at[0, 1], 5, mate)
    fwd_hi = remote(f6.at[2, 0], f6.at[2, 1], 6, mate)
    filt_mate = remote(filt_in, fx, 7, mate)
    cot_mate = remote(cm.at[1 - p], c2.at[p], 8, mate)
    for c in (pos_up, pos_dn, feat_up, feat_dn, feat_mate, filt_mate, cot_mate):
        c.start()
    c2[p] = cm[p]

    chunk = 16
    layer_x = s.astype(f32)
    xs = (pos[0:1, :] + layer_x) * (1.0 / n)
    ys = pos[1:2, :] * (1.0 / BLK_DEV)
    zs = pos[2:3, :]

    def table(i, carry):
        at = pl.multiple_of(i * chunk, chunk)
        _, a, b, c = lattice((i * chunk).astype(f32), chunk)
        cosv, sinv = turn_cos_sin(a * xs + b * ys + c * zs)
        ch, cl = halves(cosv)
        sh, sl = halves(sinv)
        th[pl.ds(at, chunk), :] = ch
        tl[pl.ds(at, chunk), :] = cl
        th[pl.ds(lat + at, chunk), :] = sh
        tl[pl.ds(lat + at, chunk), :] = sl
        return carry

    lax.fori_loop(0, lat // chunk, table, 0)
    vh, vl = halves(jnp.concatenate([fm, cmask], 0))
    two = dot_nt(th[...], jnp.concatenate([vh, vl], 0))
    full = two[:, :pair] + two[:, pair:] + dot_nt(tl[...], vh)
    ss[...] = full.reshape(n, piece, pair)

    def reduce_copy(k):
        return pltpu.make_async_remote_copy(
            src_ref=ss.at[lax.rem(s + k, n)], dst_ref=rb.at[s], send_sem=red_s.at[k],
            recv_sem=red_r.at[k], device_id=(lax.rem(s + k, n), q), device_id_type=MESH)

    def start_reduce(k, carry):
        reduce_copy(k).start()
        return carry

    feat_up.wait_recv()
    fwd_lo.start()
    feat_dn.wait_recv()
    fwd_hi.start()
    lax.fori_loop(1, n, start_reduce, 0)

    pos_up.wait_recv()
    pos_dn.wait_recv()
    pt[...] = p6[1, p].T
    loads[3].wait()
    step = 16
    part_i = cap // PARTS
    chosen = [nbr[p, e] for e in range(NB)]

    for half in range(PARTS):
        def radial(i, carry):
            at = pl.multiple_of(i * step, step)
            own = pt[pl.ds(half * part_i + at, step), :]
            for e in range(NB):
                w = chosen[e]
                far = p6[lax.div(w, BLK_DEV), lax.rem(w, BLK_DEV)]
                offset = (lax.div(w, BLK_DEV) - 1).astype(f32)
                dx = own[:, 0:1] - (far[0:1, :] + offset)
                dy = own[:, 1:2] - far[1:2, :]
                dz = own[:, 2:3] - far[2:3, :]
                sq = jnp.minimum(dx * dx + dy * dy + dz * dz, 1.0)
                left = 1.0 - sq
                u = NRAD * jnp.sqrt(sq) - 0.5
                t = jnp.exp(u)
                g = jnp.exp(-0.5 * u * u) * (0.3 * left * left)
                for r in range(NRAD):
                    if r:
                        g = g * (t * math.exp(0.5 - r))
                    a, b = halves(g)
                    gh[half, pl.ds(r * part_i + at, step), e * cap:(e + 1) * cap] = a
                    gl[half, pl.ds(r * part_i + at, step), e * cap:(e + 1) * cap] = b
            return carry

        lax.fori_loop(0, part_i // step, radial, 0)

    feat_mate.wait_recv()
    fwd_lo.wait_recv()
    fwd_hi.wait_recv()
    for layer in range(3):
        both = jnp.concatenate([f6[layer, 0], f6[layer, 1]], 0)
        for b in range(BLK_DEV):
            a, c = halves(both[:, b * cap:(b + 1) * cap].T)
            mt[layer * BLK_DEV + b] = jnp.concatenate([a, c], 1)
    for e in range(NB):
        mts[e * cap:(e + 1) * cap, :] = mt[chosen[e]]
    filt_mate.wait_recv()
    loads[5].wait()
    for r in range(NRAD):
        for i, src in enumerate((filt, fx)):
            a, b = halves(src[r])
            at = r * pair + i * panel
            fh[at:at + panel, :] = a
            fl[at:at + panel, :] = b

    pre_copies = []
    for half in range(PARTS):
        two = dot(gh[half], mts[...])
        sums = two[:, :pair] + two[:, pair:] + dot(gl[half], mts[:, :pair])
        a, b = halves(sums)
        total = None
        for r in range(NRAD):
            here = slice(r * part_i, (r + 1) * part_i)
            wh, wl = fh[r * pair:(r + 1) * pair, :], fl[r * pair:(r + 1) * pair, :]
            term = dot(jnp.concatenate([a[here], b[here]], 1), jnp.concatenate([wh, wh], 0)) + dot(a[here], wl)
            total = term if r == 0 else total + term
        for k in range(groups):
            ps[half, k] = total[:, k * pair:(k + 1) * pair]
        copies = []
        for k in range(1, groups):
            c = remote(ps.at[half, lax.rem(h + k, groups)], rx.at[half, k - 1], 16 + half * groups + k,
                       (s, lax.rem(q + 2 * k, chans)))
            c.start()
            copies.append(c)
        pre_copies.append(copies)

    def wait_reduce(k, carry):
        reduce_copy(k).wait_recv()
        return carry

    lax.fori_loop(1, n, wait_reduce, 0)
    rb[s] = ss[s]

    def add_up(k, acc):
        return acc + rb[k]

    sg[s] = lax.fori_loop(0, n, add_up, jnp.zeros((piece, pair), f32))

    def gather_copy(k):
        return pltpu.make_async_remote_copy(
            src_ref=sg.at[s], dst_ref=sg.at[s], send_sem=gat_s.at[k],
            recv_sem=gat_r.at[k], device_id=(lax.rem(s + k, n), q), device_id_type=MESH)

    def start_gather(k, carry):
        gather_copy(k).start()
        return carry

    lax.fori_loop(1, n, start_gather, 0)

    cot_mate.wait_recv()
    up_copies = []
    for half in range(PARTS):
        here = slice(half * part_i, (half + 1) * part_i)
        for c in pre_copies[half]:
            c.wait_recv()
        acc = ps[half, h]
        for k in range(1, groups):
            acc = acc + rx[half, k - 1]
        pre = acc.T
        sigma = 1.0 / (1.0 + jnp.exp(-pre))
        act = pre * sigma
        ug[half, h] = jnp.concatenate([c2[0, :, here], c2[1, :, here]], 0) * sigma * (1.0 + pre * (1.0 - sigma))
        copies = []
        for k in range(1, groups):
            c = pltpu.make_async_remote_copy(
                src_ref=ug.at[half, h], dst_ref=ug.at[half, h], send_sem=misc_s.at[16 + (PARTS + half) * groups + k],
                recv_sem=misc_r.at[16 + (PARTS + half) * groups + k],
                device_id=(s, lax.rem(q + 2 * k, chans)), device_id_type=MESH)
            c.start()
            copies.append(c)
        up_copies.append(copies)
        so[0, :, here] = act[:panel]
        so[1, :, here] = act[panel:]
    act_mate = remote(so.at[1 - p], sr, 9, mate)
    act_mate.start()

    loads[4].wait()
    f, a, b, c = lattice(0.0, lat)
    wf = wv[...].astype(f32) + MOST
    key = (wf[0:1] * SIDE + wf[1:2]) * SIDE + wf[2:3]
    hit = (key == f).astype(f32) + ((2.0 * HALF - key) == f).astype(f32)
    times = jnp.sum(hit, axis=1, keepdims=True)
    qa = a * (2.0 * math.pi / n)
    qb = b * (2.0 * math.pi / BLK_DEV)
    qc = c * (2.0 * math.pi)
    k2 = qa * qa + qb * qb + qc * qc
    raw = jnp.exp(-k2 / 2000.0) / (k2 + 100.0)
    norm = jnp.sum(times * raw * raw, axis=0, keepdims=True)
    weight = times * raw * lax.rsqrt(norm) * math.sqrt(3.0 / (n * slots))
    weight = jnp.concatenate([weight, weight], 0)

    for half in range(PARTS):
        for c in up_copies[half]:
            c.wait_recv()
        uh, ul = halves(ug[half].reshape(groups * pair, part_i))
        two = dot(fh[...], jnp.concatenate([uh, ul], 1))
        a, b = halves(two[:, :part_i] + two[:, part_i:] + dot(fl[...], uh))
        a = jnp.concatenate([a[r * pair:(r + 1) * pair] for r in range(NRAD)], 1)
        b = jnp.concatenate([b[r * pair:(r + 1) * pair] for r in range(NRAD)], 1)
        out = dot(jnp.concatenate([a, b], 0), gh[half])
        out = out[:pair] + out[pair:] + dot(a, gl[half])
        if half == 0:
            re[...] = out
        else:
            re[...] += out
    ret_mates = {}
    for layer in (0, 2, 1):
        for blk in range(BLK_DEV):
            w = layer * BLK_DEV + blk
            acc = jnp.where(chosen[0] == w, re[:, :cap], 0.0)
            for e in range(1, NB):
                acc = acc + jnp.where(chosen[e] == w, re[:, e * cap:(e + 1) * cap], 0.0)
            wo[layer, blk] = acc[:panel]
            wp[layer, blk] = acc[panel:]
        ret_mates[layer] = remote(wp.at[layer], rw.at[layer], 10 + layer, mate)
        ret_mates[layer].start()
    ret_up = remote(rt.at[1], hb.at[0], 13, nxt)
    ret_dn = remote(rt.at[0], hb.at[1], 14, prv)
    ret_mates[0].wait_recv()
    rt[0] = wo[0] + rw[0]
    ret_dn.start()
    ret_mates[2].wait_recv()
    rt[1] = wo[2] + rw[2]
    ret_up.start()

    def wait_gather(k, carry):
        gather_copy(k).wait_recv()
        return carry

    lax.fori_loop(1, n, wait_gather, 0)
    sh, sl = halves((sg[...].reshape(rows_all, pair) * weight).T)
    two = dot(jnp.concatenate([sh, sl], 0), th[...])
    far_part = two[:pair] + two[pair:] + dot(sh, tl[...])
    act_mate.wait_recv()
    mine, other = so[p], sr[...]
    first = jnp.where(p == 0, mine, other)
    second = jnp.where(p == 0, other, mine)
    upd[...] = live * (fm + jnp.concatenate([first, second], 1) + far_part[:panel])
    ret_mates[1].wait_recv()
    part = cmask + far_part[panel:] + jnp.concatenate([wo[1, b] + rw[1, b] for b in range(BLK_DEV)], 1)
    ret_up.wait_recv()
    ret_dn.wait_recv()
    grad[...] = live * (part + jnp.concatenate([hb[0, b] + hb[1, b] for b in range(BLK_DEV)], 1))

    for c in (pos_up, pos_dn, feat_up, feat_dn, feat_mate, fwd_lo, fwd_hi, filt_mate, cot_mate,
              act_mate, *ret_mates.values(), ret_up, ret_dn, *sum(pre_copies, []), *sum(up_copies, [])):
        c.wait_send()

    def drain(k, carry):
        reduce_copy(k).wait_send()
        gather_copy(k).wait_send()
        return carry

    lax.fori_loop(1, n, drain, 0)


def shards(n, chans, features, positions, counts, neighbours, wavevectors, filters, cotangent):
    panel, slots = features.shape
    cap = slots // BLK_DEV
    pair = 2 * panel
    groups = chans // 2
    piece = -(-(-(-2 * HALF // n)) // 8) * 8
    while (n * piece) % 32:
        piece += 8
    rows = n * piece
    part_i = cap // PARTS
    vm = pltpu.VMEM
    sm = pltpu.SMEM
    scratch = [
        vm(features.shape, f32),
        vm(positions.shape, f32),
        sm(counts.shape, jnp.int32),
        sm(neighbours.shape, jnp.int32),
        vm(wavevectors.shape, jnp.int32),
        vm(filters.shape, f32),
        vm(cotangent.shape, f32),
        vm((3, 2, panel, slots), f32),
        vm((3, BLK_DEV, 8, cap), f32),
        vm((cap, 8), f32),
        vm(filters.shape, f32),
        vm((NRAD * pair, groups * pair), bf16),
        vm((NRAD * pair, groups * pair), bf16),
        vm((BLK_DEV, panel, cap), f32),
        vm((2, panel, cap), f32),
        vm((PARTS, NRAD * part_i, NB * cap), bf16),
        vm((PARTS, NRAD * part_i, NB * cap), bf16),
        vm((NB * cap, 2 * pair), bf16),
        vm((3 * BLK_DEV, cap, 2 * pair), bf16),
        vm((rows, slots), bf16),
        vm((rows, slots), bf16),
        vm((n, piece, pair), f32),
        vm((n, piece, pair), f32),
        vm((n, piece, pair), f32),
        vm((PARTS, groups, part_i, pair), f32),
        vm((PARTS, max(groups - 1, 1), part_i, pair), f32),
        vm((PARTS, groups, pair, part_i), f32),
        vm((2, panel, cap), f32),
        vm((panel, cap), f32),
        vm((pair, NB * cap), f32),
        vm((3, BLK_DEV, panel, cap), f32),
        vm((3, BLK_DEV, panel, cap), f32),
        vm((3, BLK_DEV, panel, cap), f32),
        vm((2, BLK_DEV, panel, cap), f32),
        vm((2, BLK_DEV, panel, cap), f32),
        pltpu.SemaphoreType.DMA((7,)),
        pltpu.SemaphoreType.DMA((16 + 2 * PARTS * groups,)),
        pltpu.SemaphoreType.DMA((16 + 2 * PARTS * groups,)),
        pltpu.SemaphoreType.DMA((n,)),
        pltpu.SemaphoreType.DMA((n,)),
        pltpu.SemaphoreType.DMA((n,)),
        pltpu.SemaphoreType.DMA((n,)),
    ]
    whole = pl.BlockSpec(memory_space=pltpu.VMEM)
    anywhere = pl.BlockSpec(memory_space=pl.ANY)
    out = jax.ShapeDtypeStruct((panel, slots), f32)
    return pl.pallas_call(
        functools.partial(kernel, n, chans),
        out_shape=(out, out),
        in_specs=[anywhere] * 7,
        out_specs=(whole, whole),
        scratch_shapes=scratch,
        compiler_params=pltpu.CompilerParams(
            collective_id=0, has_side_effects=True, vmem_limit_bytes=60 * 1024 * 1024),
    )(features, positions, counts, neighbours, wavevectors, filters, cotangent)


def solution(mesh):
    return jax.shard_map(
        functools.partial(shards, mesh.shape["space"], mesh.shape["chan"]),
        mesh=mesh,
        in_specs=(
            P("chan", "space"),
            P(None, "space"),
            P("space"),
            P("space", None),
            P(),
            P(None, "chan", None),
            P("chan", "space"),
        ),
        out_specs=(P("chan", "space"), P("chan", "space")),
        check_vma=False,
    )
```

time: 55 us -> 42.5 us (0.77)
  Pallas kernels: 47.2 us -> 39.4 us
  local copies, waits for them, and re-layouts: 6.88 us -> 2.26 us
    pallas_call x1, Pallas kernels: 47.2 us -> 39.4 us  [shards(): pl.pallas_call(functools.partial(kernel, n, chans), out_shape=(out, out),...]
    unnamed x16 -> x4, local copies, waits for them, and re-layouts: 6.88 us -> 2.26 us
where the time goes in v1:
time: 42.5 us; the launch traced here: 42.3 us
  Pallas kernels  39.4 us (93%)
  local copies, waits for them, and re-layouts  2.26 us (5%)
  between operations  0.65 us (2%)
    pallas_call x1, Pallas kernels, shards(): pl.pallas_call(functools.partial(kernel, n, chans), out_shape=(out, out),...  39.4 us
    unnamed x4, local copies, waits for them, and re-layouts  2.26 us

profile of v1, /device:TPU:0, one launch (start us, length us, event | category | flops | bytes accessed | tf_op | source)
XLA Modules:
  0.0 42.3 jit_solution(18049608775275284565)
XLA Ops:
  0.6 39.4 %shard_map.86 = (f32[64,512]{1,0:T(8,128)}, f32[64,512]{1,0:T(8,128)}) custom-call(f32[64,512]{1,0:T(8,128)} %feat_in.1, f32[3,512]{1,0:T(4,128)} %pos_in.1, s32[2]{0:T(128)} %counts_in.1, s32[2,4]{1,0:T(2,128)} %nbr_in.1, s32[3,512]{1,0:T(4,128)} %wv_in.1, f32[8,64,256]{2,1,0:T(8,128)} %filt_in.1, f32[64,512]{1,0:T(8,128)} %cot_in.1), custom_call_target="tpu_custom_call" | custom-call | tf_op jit(solution)/shard_map/pallas_call | solution.py:432
  40.0 0.0 copy-start
  40.0 1.6 %copy.11 = f32[64,512]{1,0:T(8,128)} copy(f32[64,512]{1,0:T(8,128)} %get-tuple-element.4) | data formatting | bytes 262144
  41.6 0.0 copy-done
  41.6 0.7 %copy.12 = f32[64,512]{1,0:T(8,128)} copy(f32[64,512]{1,0:T(8,128)S(1)} %copy-done) | data formatting | bytes 262144
Async XLA Ops:
  40.0 1.6 %copy-start = (f32[64,512]{1,0:T(8,128)S(1)}, f32[64,512]{1,0:T(8,128)}, u32[]{:S(2)}) copy-start(f32[64,512]{1,0:T(8,128)} %get-tuple-element.5) | copy-start | bytes 393220

commit v2 on v1

--- a/solution.py
+++ b/solution.py
@@ -55,7 +55,7 @@
     return f, a - MOST, b - MOST, c - MOST
 
 
-def kernel(n, chans, feat_in, pos_in, counts_in, nbr_in, wv_in, filt_in, cot_in, upd, grad,
+def kernel(n, chans, feat_in, pos_in, counts_in, nbr_in, wv_in, filt_in, cot_in, upd, grad, live_out,
            feat, pos, counts, nbr, wv, filt, cot,
            f6, p6, pt, fx, fh, fl, cm, c2, gh, gl, mts, mt, th, tl, ss, rb, sg, ps, rx, ug, so, sr,
            re, wo, wp, rw, rt, hb, load_s, misc_s, misc_r, red_s, red_r, gat_s, gat_r):
@@ -160,10 +160,6 @@
         reduce_copy(k).start()
         return carry
 
-    feat_up.wait_recv()
-    fwd_lo.start()
-    feat_dn.wait_recv()
-    fwd_hi.start()
     lax.fori_loop(1, n, start_reduce, 0)
 
     pos_up.wait_recv()
@@ -199,6 +195,11 @@
             return carry
 
         lax.fori_loop(0, part_i // step, radial, 0)
+        if half == 0:
+            feat_up.wait_recv()
+            fwd_lo.start()
+            feat_dn.wait_recv()
+            fwd_hi.start()
 
     feat_mate.wait_recv()
     fwd_lo.wait_recv()
@@ -239,29 +240,6 @@
             c.start()
             copies.append(c)
         pre_copies.append(copies)
-
-    def wait_reduce(k, carry):
-        reduce_copy(k).wait_recv()
-        return carry
-
-    lax.fori_loop(1, n, wait_reduce, 0)
-    rb[s] = ss[s]
-
-    def add_up(k, acc):
-        return acc + rb[k]
-
-    sg[s] = lax.fori_loop(0, n, add_up, jnp.zeros((piece, pair), f32))
-
-    def gather_copy(k):
-        return pltpu.make_async_remote_copy(
-            src_ref=sg.at[s], dst_ref=sg.at[s], send_sem=gat_s.at[k],
-            recv_sem=gat_r.at[k], device_id=(lax.rem(s + k, n), q), device_id_type=MESH)
-
-    def start_gather(k, carry):
-        gather_copy(k).start()
-        return carry
-
-    lax.fori_loop(1, n, start_gather, 0)
 
     cot_mate.wait_recv()
     up_copies = []
@@ -290,6 +268,29 @@
     act_mate = remote(so.at[1 - p], sr, 9, mate)
     act_mate.start()
 
+    def wait_reduce(k, carry):
+        reduce_copy(k).wait_recv()
+        return carry
+
+    lax.fori_loop(1, n, wait_reduce, 0)
+    rb[s] = ss[s]
+
+    def add_up(k, acc):
+        return acc + rb[k]
+
+    sg[s] = lax.fori_loop(0, n, add_up, jnp.zeros((piece, pair), f32))
+
+    def gather_copy(k):
+        return pltpu.make_async_remote_copy(
+            src_ref=sg.at[s], dst_ref=sg.at[s], send_sem=gat_s.at[k],
+            recv_sem=gat_r.at[k], device_id=(lax.rem(s + k, n), q), device_id_type=MESH)
+
+    def start_gather(k, carry):
+        gather_copy(k).start()
+        return carry
+
+    lax.fori_loop(1, n, start_gather, 0)
+
     loads[4].wait()
     f, a, b, c = lattice(0.0, lat)
     wf = wv[...].astype(f32) + MOST
@@ -305,6 +306,7 @@
     weight = times * raw * lax.rsqrt(norm) * math.sqrt(3.0 / (n * slots))
     weight = jnp.concatenate([weight, weight], 0)
 
+    pair_cots = []
     for half in range(PARTS):
         for c in up_copies[half]:
             c.wait_recv()
@@ -313,23 +315,37 @@
         a, b = halves(two[:, :part_i] + two[:, part_i:] + dot(fl[...], uh))
         a = jnp.concatenate([a[r * pair:(r + 1) * pair] for r in range(NRAD)], 1)
         b = jnp.concatenate([b[r * pair:(r + 1) * pair] for r in range(NRAD)], 1)
-        out = dot(jnp.concatenate([a, b], 0), gh[half])
-        out = out[:pair] + out[pair:] + dot(a, gl[half])
+        both = jnp.concatenate([a, b], 0)
+        pair_cots.append((a, both))
+        out = dot(both, gh[half, :, cap:])
+        out = out[:pair] + out[pair:] + dot(a, gl[half, :, cap:])
         if half == 0:
-            re[...] = out
+            re[:, cap:] = out
         else:
-            re[...] += out
+            re[:, cap:] += out
     ret_mates = {}
-    for layer in (0, 2, 1):
+
+    def window_sums(layer, entries):
         for blk in range(BLK_DEV):
             w = layer * BLK_DEV + blk
-            acc = jnp.where(chosen[0] == w, re[:, :cap], 0.0)
-            for e in range(1, NB):
-                acc = acc + jnp.where(chosen[e] == w, re[:, e * cap:(e + 1) * cap], 0.0)
+            acc = None
+            for e in entries:
+                term = jnp.where(chosen[e] == w, re[:, e * cap:(e + 1) * cap], 0.0)
+                acc = term if acc is None else acc + term
             wo[layer, blk] = acc[:panel]
             wp[layer, blk] = acc[panel:]
         ret_mates[layer] = remote(wp.at[layer], rw.at[layer], 10 + layer, mate)
         ret_mates[layer].start()
+
+    window_sums(0, range(1, NB))
+    window_sums(2, range(1, NB))
+    out = None
+    for half in range(PARTS):
+        a, both = pair_cots[half]
+        term = dot(both, gh[half, :, :cap])
+        term = term[:pair] + term[pair:] + dot(a, gl[half, :, :cap])
+        out = term if half == 0 else out + term
+    re[:, :cap] = out
     ret_up = remote(rt.at[1], hb.at[0], 13, nxt)
     ret_dn = remote(rt.at[0], hb.at[1], 14, prv)
     ret_mates[0].wait_recv()
@@ -338,6 +354,7 @@
     ret_mates[2].wait_recv()
     rt[1] = wo[2] + rw[2]
     ret_up.start()
+    window_sums(1, range(NB))
 
     def wait_gather(k, carry):
         gather_copy(k).wait_recv()
@@ -351,12 +368,13 @@
     mine, other = so[p], sr[...]
     first = jnp.where(p == 0, mine, other)
     second = jnp.where(p == 0, other, mine)
-    upd[...] = live * (fm + jnp.concatenate([first, second], 1) + far_part[:panel])
+    live_out[...] = jnp.broadcast_to(live, live_out.shape)
+    upd[...] = (fm + jnp.concatenate([first, second], 1) + far_part[:panel])
     ret_mates[1].wait_recv()
     part = cmask + far_part[panel:] + jnp.concatenate([wo[1, b] + rw[1, b] for b in range(BLK_DEV)], 1)
     ret_up.wait_recv()
     ret_dn.wait_recv()
-    grad[...] = live * (part + jnp.concatenate([hb[0, b] + hb[1, b] for b in range(BLK_DEV)], 1))
+    grad[...] = (part + jnp.concatenate([hb[0, b] + hb[1, b] for b in range(BLK_DEV)], 1))
 
     for c in (pos_up, pos_dn, feat_up, feat_dn, feat_mate, fwd_lo, fwd_hi, filt_mate, cot_mate,
               act_mate, *ret_mates.values(), ret_up, ret_dn, *sum(pre_copies, []), *sum(up_copies, [])):
@@ -429,15 +447,16 @@
     whole = pl.BlockSpec(memory_space=pltpu.VMEM)
     anywhere = pl.BlockSpec(memory_space=pl.ANY)
     out = jax.ShapeDtypeStruct((panel, slots), f32)
-    return pl.pallas_call(
+    upd, grad, live = pl.pallas_call(
         functools.partial(kernel, n, chans),
-        out_shape=(out, out),
+        out_shape=(out, out, out),
         in_specs=[anywhere] * 7,
-        out_specs=(whole, whole),
+        out_specs=(whole, whole, whole),
         scratch_shapes=scratch,
         compiler_params=pltpu.CompilerParams(
             collective_id=0, has_side_effects=True, vmem_limit_bytes=60 * 1024 * 1024),
     )(features, positions, counts, neighbours, wavevectors, filters, cotangent)
+    return upd * live, grad * live
 
 
 def solution(mesh):

time: 42.5 us -> 43.1 us (1.014)
  local copies, waits for them, and re-layouts: 2.26 us -> 0 us
  other arithmetic: 0 us -> 1.76 us
  Pallas kernels: 39.4 us -> 40.5 us
    unnamed x4 -> x0, local copies, waits for them, and re-layouts: 2.26 us -> none
    mul x0 -> x1, other arithmetic: none -> 1.76 us  [shards(): return (upd * live, grad * live)]
    pallas_call x1, Pallas kernels: 39.4 us -> 40.5 us  [shards(): pl.pallas_call(functools.partial(kernel, n, chans), out_shape=(out, out,...]
where the time goes in v2:
time: 43.1 us; the launch traced here: 42.9 us
  Pallas kernels  40.5 us (94%)
  other arithmetic  1.76 us (4%)
  between operations  0.64 us (1%)
    pallas_call x1, Pallas kernels, shards(): pl.pallas_call(functools.partial(kernel, n, chans), out_shape=(out, out,...  40.5 us
    mul x1, other arithmetic, shards(): return (upd * live, grad * live)  1.76 us

profile of v2, /device:TPU:0, one launch (start us, length us, event | category | flops | bytes accessed | tf_op | source)
XLA Modules:
  0.0 42.9 jit_solution(13285840612332133752)
XLA Ops:
  0.6 40.5 %shard_map.86 = (f32[64,512]{1,0:T(8,128)}, f32[64,512]{1,0:T(8,128)}, f32[64,512]{1,0:T(8,128)}) custom-call(f32[64,512]{1,0:T(8,128)} %feat_in.1, f32[3,512]{1,0:T(4,128)} %pos_in.1, s32[2]{0:T(128)} %counts_in.1, s32[2,4]{1,0:T(2,128)} %nbr_in.1, s32[3,512]{1,0:T(4,128)} %wv_in.1, f32[8,64,256]{2,1,0:T(8,128)} %filt_in.1, f32[64,512]{1,0:T(8,128)} %cot_in.1), custom_call_target="tpu_custom_call" | custom-call | tf_op jit(solution)/shard_map/pallas_call | solution.py:450
  41.2 1.8 %fusion = (f32[64,512]{1,0:T(8,128)}, f32[64,512]{1,0:T(8,128)}) fusion(f32[64,512]{1,0:T(8,128)} %get-tuple-element.7, f32[64,512]{1,0:T(8,128)} %get-tuple-element.6, f32[64,512]{1,0:T(8,128)} %get-tuple-element.5), kind=kLoop, calls=%fused_computation | loop fusion | flops 65536 | bytes 655360 | tf_op jit(solution)/shard_map/mul | solution.py:459

commit v3 on v2

--- a/solution.py
+++ b/solution.py
@@ -57,7 +57,7 @@
 
 def kernel(n, chans, feat_in, pos_in, counts_in, nbr_in, wv_in, filt_in, cot_in, upd, grad, live_out,
            feat, pos, counts, nbr, wv, filt, cot,
-           f6, p6, pt, fx, fh, fl, cm, c2, gh, gl, mts, mt, th, tl, ss, rb, sg, ps, rx, ug, so, sr,
+           f6, p6, pt, fx, fh, fl, cm, c2, gh, gl, mts, mt, vs, th, tl, ss, rb, sg, ps, rx, ug, so, sr,
            re, wo, wp, rw, rt, hb, load_s, misc_s, misc_r, red_s, red_r, gat_s, gat_r):
     loads = [
         pltpu.make_async_copy(a, b, load_s.at[i])
@@ -69,9 +69,9 @@
         c.start()
     panel, slots = feat.shape
     cap = slots // BLK_DEV
-    rows_all = th.shape[0]
-    lat = rows_all // 2
     piece = ss.shape[1]
+    grain = piece // 2
+    rows_all = n * piece
     pair = 2 * panel
     groups = chans // 2
     s = lax.axis_index("space")
@@ -133,34 +133,31 @@
     ys = pos[1:2, :] * (1.0 / BLK_DEV)
     zs = pos[2:3, :]
 
-    def table(i, carry):
-        at = pl.multiple_of(i * chunk, chunk)
-        _, a, b, c = lattice((i * chunk).astype(f32), chunk)
-        cosv, sinv = turn_cos_sin(a * xs + b * ys + c * zs)
-        ch, cl = halves(cosv)
-        sh, sl = halves(sinv)
-        th[pl.ds(at, chunk), :] = ch
-        tl[pl.ds(at, chunk), :] = cl
-        th[pl.ds(lat + at, chunk), :] = sh
-        tl[pl.ds(lat + at, chunk), :] = sl
-        return carry
-
-    lax.fori_loop(0, lat // chunk, table, 0)
-    vh, vl = halves(jnp.concatenate([fm, cmask], 0))
-    two = dot_nt(th[...], jnp.concatenate([vh, vl], 0))
-    full = two[:, :pair] + two[:, pair:] + dot_nt(tl[...], vh)
-    ss[...] = full.reshape(n, piece, pair)
-
     def reduce_copy(k):
         return pltpu.make_async_remote_copy(
             src_ref=ss.at[lax.rem(s + k, n)], dst_ref=rb.at[s], send_sem=red_s.at[k],
             recv_sem=red_r.at[k], device_id=(lax.rem(s + k, n), q), device_id_type=MESH)
 
-    def start_reduce(k, carry):
-        reduce_copy(k).start()
+    vh, vl = halves(jnp.concatenate([fm, cmask], 0))
+    vs[...] = jnp.concatenate([vh, vl], 0)
+
+    def send_piece(k, carry):
+        to = lax.rem(s + k, n)
+        for at in range(0, grain, chunk):
+            _, a, b, c = lattice((to * grain + at).astype(f32), chunk)
+            cosv, sinv = turn_cos_sin(a * xs + b * ys + c * zs)
+            th[to, at:at + chunk, :], tl[to, at:at + chunk, :] = halves(cosv)
+            th[to, grain + at:grain + at + chunk, :], tl[to, grain + at:grain + at + chunk, :] = halves(sinv)
+        two = dot_nt(th[to], vs[...])
+        ss[to] = two[:, :pair] + two[:, pair:] + dot_nt(tl[to], vs[:pair, :])
+
+        @pl.when(k < n)
+        def _():
+            reduce_copy(k).start()
+
         return carry
 
-    lax.fori_loop(1, n, start_reduce, 0)
+    lax.fori_loop(1, n + 1, send_piece, 0)
 
     pos_up.wait_recv()
     pos_dn.wait_recv()
@@ -220,6 +217,30 @@
             fh[at:at + panel, :] = a
             fl[at:at + panel, :] = b
 
+    def gather_copy(k):
+        return pltpu.make_async_remote_copy(
+            src_ref=sg.at[s], dst_ref=sg.at[s], send_sem=gat_s.at[k],
+            recv_sem=gat_r.at[k], device_id=(lax.rem(s + k, n), q), device_id_type=MESH)
+
+    def all_gather_start():
+        def wait_reduce(k, carry):
+            reduce_copy(k).wait_recv()
+            return carry
+
+        lax.fori_loop(1, n, wait_reduce, 0)
+        rb[s] = ss[s]
+
+        def add_up(k, acc):
+            return acc + rb[k]
+
+        sg[s] = lax.fori_loop(0, n, add_up, jnp.zeros((piece, pair), f32))
+
+        def start_gather(k, carry):
+            gather_copy(k).start()
+            return carry
+
+        lax.fori_loop(1, n, start_gather, 0)
+
     pre_copies = []
     for half in range(PARTS):
         two = dot(gh[half], mts[...])
@@ -240,6 +261,8 @@
             c.start()
             copies.append(c)
         pre_copies.append(copies)
+        if half == 0:
+            all_gather_start()
 
     cot_mate.wait_recv()
     up_copies = []
@@ -268,31 +291,8 @@
     act_mate = remote(so.at[1 - p], sr, 9, mate)
     act_mate.start()
 
-    def wait_reduce(k, carry):
-        reduce_copy(k).wait_recv()
-        return carry
-
-    lax.fori_loop(1, n, wait_reduce, 0)
-    rb[s] = ss[s]
-
-    def add_up(k, acc):
-        return acc + rb[k]
-
-    sg[s] = lax.fori_loop(0, n, add_up, jnp.zeros((piece, pair), f32))
-
-    def gather_copy(k):
-        return pltpu.make_async_remote_copy(
-            src_ref=sg.at[s], dst_ref=sg.at[s], send_sem=gat_s.at[k],
-            recv_sem=gat_r.at[k], device_id=(lax.rem(s + k, n), q), device_id_type=MESH)
-
-    def start_gather(k, carry):
-        gather_copy(k).start()
-        return carry
-
-    lax.fori_loop(1, n, start_gather, 0)
-
     loads[4].wait()
-    f, a, b, c = lattice(0.0, lat)
+    f, a, b, c = lattice(0.0, n * grain)
     wf = wv[...].astype(f32) + MOST
     key = (wf[0:1] * SIDE + wf[1:2]) * SIDE + wf[2:3]
     hit = (key == f).astype(f32) + ((2.0 * HALF - key) == f).astype(f32)
@@ -304,7 +304,8 @@
     raw = jnp.exp(-k2 / 2000.0) / (k2 + 100.0)
     norm = jnp.sum(times * raw * raw, axis=0, keepdims=True)
     weight = times * raw * lax.rsqrt(norm) * math.sqrt(3.0 / (n * slots))
-    weight = jnp.concatenate([weight, weight], 0)
+    weight = weight.reshape(n, grain, 1)
+    weight = jnp.concatenate([weight, weight], 1).reshape(rows_all, 1)
 
     pair_cots = []
     for half in range(PARTS):
@@ -362,8 +363,8 @@
 
     lax.fori_loop(1, n, wait_gather, 0)
     sh, sl = halves((sg[...].reshape(rows_all, pair) * weight).T)
-    two = dot(jnp.concatenate([sh, sl], 0), th[...])
-    far_part = two[:pair] + two[pair:] + dot(sh, tl[...])
+    two = dot(jnp.concatenate([sh, sl], 0), th[...].reshape(rows_all, slots))
+    far_part = two[:pair] + two[pair:] + dot(sh, tl[...].reshape(rows_all, slots))
     act_mate.wait_recv()
     mine, other = so[p], sr[...]
     first = jnp.where(p == 0, mine, other)
@@ -393,10 +394,7 @@
     cap = slots // BLK_DEV
     pair = 2 * panel
     groups = chans // 2
-    piece = -(-(-(-2 * HALF // n)) // 8) * 8
-    while (n * piece) % 32:
-        piece += 8
-    rows = n * piece
+    piece = -(-(-(-2 * HALF // n)) // 32) * 32
     part_i = cap // PARTS
     vm = pltpu.VMEM
     sm = pltpu.SMEM
@@ -420,8 +418,9 @@
         vm((PARTS, NRAD * part_i, NB * cap), bf16),
         vm((NB * cap, 2 * pair), bf16),
         vm((3 * BLK_DEV, cap, 2 * pair), bf16),
-        vm((rows, slots), bf16),
-        vm((rows, slots), bf16),
+        vm((2 * pair, slots), bf16),
+        vm((n, piece, slots), bf16),
+        vm((n, piece, slots), bf16),
         vm((n, piece, pair), f32),
         vm((n, piece, pair), f32),
         vm((n, piece, pair), f32),

time: 43.1 us -> 44.3 us (1.028)
  Pallas kernels: 40.5 us -> 41.7 us
    pallas_call x1, Pallas kernels: 40.5 us -> 41.7 us  [shards(): pl.pallas_call(functools.partial(kernel, n, chans), out_shape=(out, out,...]
where the time goes in v3:
time: 44.3 us; the launch traced here: 44.1 us
  Pallas kernels  41.7 us (94%)
  other arithmetic  1.76 us (4%)
  between operations  0.64 us (1%)
    pallas_call x1, Pallas kernels, shards(): pl.pallas_call(functools.partial(kernel, n, chans), out_shape=(out, out,...  41.7 us
    mul x1, other arithmetic, shards(): return (upd * live, grad * live)  1.76 us

profile of v3, /device:TPU:0, one launch (start us, length us, event | category | flops | bytes accessed | tf_op | source)
XLA Modules:
  0.0 44.1 jit_solution(6904921295237860407)
XLA Ops:
  0.6 41.7 %shard_map.86 = (f32[64,512]{1,0:T(8,128)}, f32[64,512]{1,0:T(8,128)}, f32[64,512]{1,0:T(8,128)}) custom-call(f32[64,512]{1,0:T(8,128)} %feat_in.1, f32[3,512]{1,0:T(4,128)} %pos_in.1, s32[2]{0:T(128)} %counts_in.1, s32[2,4]{1,0:T(2,128)} %nbr_in.1, s32[3,512]{1,0:T(4,128)} %wv_in.1, f32[8,64,256]{2,1,0:T(8,128)} %filt_in.1, f32[64,512]{1,0:T(8,128)} %cot_in.1), custom_call_target="tpu_custom_call" | custom-call | tf_op jit(solution)/shard_map/pallas_call | solution.py:449
  42.4 1.8 %fusion = (f32[64,512]{1,0:T(8,128)}, f32[64,512]{1,0:T(8,128)}) fusion(f32[64,512]{1,0:T(8,128)} %get-tuple-element.7, f32[64,512]{1,0:T(8,128)} %get-tuple-element.6, f32[64,512]{1,0:T(8,128)} %get-tuple-element.5), kind=kLoop, calls=%fused_computation | loop fusion | flops 65536 | bytes 655360 | tf_op jit(solution)/shard_map/mul | solution.py:458

commit v4 on v3

--- a/solution.py
+++ b/solution.py
@@ -27,10 +27,6 @@
 
 def dot(a, b):
     return jnp.dot(a, b, preferred_element_type=f32)
-
-
-def dot_nt(a, b):
-    return lax.dot_general(a, b, (((1,), (1,)), ((), ())), preferred_element_type=f32)
 
 
 def turn_cos_sin(p):
@@ -112,6 +108,31 @@
     for b in range(BLK_DEV):
         p6[1, b, 0:3, :] = pos[:, b * cap:(b + 1) * cap]
 
+    def split_filters(src, i):
+        for r in range(NRAD):
+            a, b = halves(src[r] * math.exp(-0.5 * r * r))
+            at = r * pair + i * panel
+            fh[at:at + panel, :] = a
+            fl[at:at + panel, :] = b
+
+    loads[5].wait()
+    split_filters(filt, 0)
+    loads[4].wait()
+    f, a, b, c = lattice(0.0, n * grain)
+    wf = wv[...].astype(f32) + MOST
+    key = (wf[0:1] * SIDE + wf[1:2]) * SIDE + wf[2:3]
+    hit = (key == f).astype(f32) + ((2.0 * HALF - key) == f).astype(f32)
+    times = jnp.sum(hit, axis=1, keepdims=True)
+    qa = a * (2.0 * math.pi / n)
+    qb = b * (2.0 * math.pi / BLK_DEV)
+    qc = c * (2.0 * math.pi)
+    k2 = qa * qa + qb * qb + qc * qc
+    raw = jnp.exp(-k2 / 2000.0) / (k2 + 100.0)
+    norm = jnp.sum(times * raw * raw, axis=0, keepdims=True)
+    weight = times * raw * lax.rsqrt(norm) * math.sqrt(3.0 / (n * slots))
+    weight = weight.reshape(n, grain, 1)
+    weight = jnp.concatenate([weight, weight], 1).reshape(rows_all, 1)
+
     pl.semaphore_wait(barrier, n - 1 + 1 + groups - 1)
 
     pos_up = remote(p6.at[1], p6.at[0], 0, nxt)
@@ -138,8 +159,7 @@
             src_ref=ss.at[lax.rem(s + k, n)], dst_ref=rb.at[s], send_sem=red_s.at[k],
             recv_sem=red_r.at[k], device_id=(lax.rem(s + k, n), q), device_id_type=MESH)
 
-    vh, vl = halves(jnp.concatenate([fm, cmask], 0))
-    vs[...] = jnp.concatenate([vh, vl], 0)
+    vs[...] = jnp.concatenate(halves(jnp.concatenate([fm, cmask], 0).T), 1)
 
     def send_piece(k, carry):
         to = lax.rem(s + k, n)
@@ -148,8 +168,8 @@
             cosv, sinv = turn_cos_sin(a * xs + b * ys + c * zs)
             th[to, at:at + chunk, :], tl[to, at:at + chunk, :] = halves(cosv)
             th[to, grain + at:grain + at + chunk, :], tl[to, grain + at:grain + at + chunk, :] = halves(sinv)
-        two = dot_nt(th[to], vs[...])
-        ss[to] = two[:, :pair] + two[:, pair:] + dot_nt(tl[to], vs[:pair, :])
+        two = dot(th[to], vs[...])
+        ss[to] = two[:, :pair] + two[:, pair:] + dot(tl[to], vs[:, :pair])
 
         @pl.when(k < n)
         def _():
@@ -185,7 +205,7 @@
                 g = jnp.exp(-0.5 * u * u) * (0.3 * left * left)
                 for r in range(NRAD):
                     if r:
-                        g = g * (t * math.exp(0.5 - r))
+                        g = g * t
                     a, b = halves(g)
                     gh[half, pl.ds(r * part_i + at, step), e * cap:(e + 1) * cap] = a
                     gl[half, pl.ds(r * part_i + at, step), e * cap:(e + 1) * cap] = b
@@ -197,6 +217,9 @@
             fwd_lo.start()
             feat_dn.wait_recv()
             fwd_hi.start()
+
+    filt_mate.wait_recv()
+    split_filters(fx, 1)
 
     feat_mate.wait_recv()
     fwd_lo.wait_recv()
@@ -208,15 +231,6 @@
             mt[layer * BLK_DEV + b] = jnp.concatenate([a, c], 1)
     for e in range(NB):
         mts[e * cap:(e + 1) * cap, :] = mt[chosen[e]]
-    filt_mate.wait_recv()
-    loads[5].wait()
-    for r in range(NRAD):
-        for i, src in enumerate((filt, fx)):
-            a, b = halves(src[r])
-            at = r * pair + i * panel
-            fh[at:at + panel, :] = a
-            fl[at:at + panel, :] = b
-
     def gather_copy(k):
         return pltpu.make_async_remote_copy(
             src_ref=sg.at[s], dst_ref=sg.at[s], send_sem=gat_s.at[k],
@@ -261,8 +275,8 @@
             c.start()
             copies.append(c)
         pre_copies.append(copies)
-        if half == 0:
-            all_gather_start()
+
+    all_gather_start()
 
     cot_mate.wait_recv()
     up_copies = []
@@ -290,22 +304,6 @@
         so[1, :, here] = act[panel:]
     act_mate = remote(so.at[1 - p], sr, 9, mate)
     act_mate.start()
-
-    loads[4].wait()
-    f, a, b, c = lattice(0.0, n * grain)
-    wf = wv[...].astype(f32) + MOST
-    key = (wf[0:1] * SIDE + wf[1:2]) * SIDE + wf[2:3]
-    hit = (key == f).astype(f32) + ((2.0 * HALF - key) == f).astype(f32)
-    times = jnp.sum(hit, axis=1, keepdims=True)
-    qa = a * (2.0 * math.pi / n)
-    qb = b * (2.0 * math.pi / BLK_DEV)
-    qc = c * (2.0 * math.pi)
-    k2 = qa * qa + qb * qb + qc * qc
-    raw = jnp.exp(-k2 / 2000.0) / (k2 + 100.0)
-    norm = jnp.sum(times * raw * raw, axis=0, keepdims=True)
-    weight = times * raw * lax.rsqrt(norm) * math.sqrt(3.0 / (n * slots))
-    weight = weight.reshape(n, grain, 1)
-    weight = jnp.concatenate([weight, weight], 1).reshape(rows_all, 1)
 
     pair_cots = []
     for half in range(PARTS):
@@ -418,7 +416,7 @@
         vm((PARTS, NRAD * part_i, NB * cap), bf16),
         vm((NB * cap, 2 * pair), bf16),
         vm((3 * BLK_DEV, cap, 2 * pair), bf16),
-        vm((2 * pair, slots), bf16),
+        vm((slots, 2 * pair), bf16),
         vm((n, piece, slots), bf16),
         vm((n, piece, slots), bf16),
         vm((n, piece, pair), f32),

time: 44.3 us -> 43.5 us (0.982)
  Pallas kernels: 41.7 us -> 40.9 us
    pallas_call x1, Pallas kernels: 41.7 us -> 40.9 us  [shards(): pl.pallas_call(functools.partial(kernel, n, chans), out_shape=(out, out,...]
where the time goes in v4:
time: 43.5 us; the launch traced here: 43.3 us
  Pallas kernels  40.9 us (94%)
  other arithmetic  1.76 us (4%)
  between operations  0.64 us (1%)
    pallas_call x1, Pallas kernels, shards(): pl.pallas_call(functools.partial(kernel, n, chans), out_shape=(out, out,...  40.9 us
    mul x1, other arithmetic, shards(): return (upd * live, grad * live)  1.76 us

profile of v4, /device:TPU:0, one launch (start us, length us, event | category | flops | bytes accessed | tf_op | source)
XLA Modules:
  0.0 43.3 jit_solution(18429786753735541768)
XLA Ops:
  0.6 40.9 %shard_map.86 = (f32[64,512]{1,0:T(8,128)}, f32[64,512]{1,0:T(8,128)}, f32[64,512]{1,0:T(8,128)}) custom-call(f32[64,512]{1,0:T(8,128)} %feat_in.1, f32[3,512]{1,0:T(4,128)} %pos_in.1, s32[2]{0:T(128)} %counts_in.1, s32[2,4]{1,0:T(2,128)} %nbr_in.1, s32[3,512]{1,0:T(4,128)} %wv_in.1, f32[8,64,256]{2,1,0:T(8,128)} %filt_in.1, f32[64,512]{1,0:T(8,128)} %cot_in.1), custom_call_target="tpu_custom_call" | custom-call | tf_op jit(solution)/shard_map/pallas_call | solution.py:447
  41.6 1.8 %fusion = (f32[64,512]{1,0:T(8,128)}, f32[64,512]{1,0:T(8,128)}) fusion(f32[64,512]{1,0:T(8,128)} %get-tuple-element.7, f32[64,512]{1,0:T(8,128)} %get-tuple-element.6, f32[64,512]{1,0:T(8,128)} %get-tuple-element.5), kind=kLoop, calls=%fused_computation | loop fusion | flops 65536 | bytes 655360 | tf_op jit(solution)/shard_map/mul | solution.py:456

commit v5 on v4

--- a/solution.py
+++ b/solution.py
@@ -161,8 +161,7 @@
 
     vs[...] = jnp.concatenate(halves(jnp.concatenate([fm, cmask], 0).T), 1)
 
-    def send_piece(k, carry):
-        to = lax.rem(s + k, n)
+    def piece_sums(to, carry):
         for at in range(0, grain, chunk):
             _, a, b, c = lattice((to * grain + at).astype(f32), chunk)
             cosv, sinv = turn_cos_sin(a * xs + b * ys + c * zs)
@@ -170,14 +169,13 @@
             th[to, grain + at:grain + at + chunk, :], tl[to, grain + at:grain + at + chunk, :] = halves(sinv)
         two = dot(th[to], vs[...])
         ss[to] = two[:, :pair] + two[:, pair:] + dot(tl[to], vs[:, :pair])
-
-        @pl.when(k < n)
-        def _():
-            reduce_copy(k).start()
-
         return carry
 
-    lax.fori_loop(1, n + 1, send_piece, 0)
+    lax.fori_loop(0, n, piece_sums, 0)
+
+    def start_reduce(k, carry):
+        reduce_copy(k).start()
+        return carry
 
     pos_up.wait_recv()
     pos_dn.wait_recv()
@@ -217,6 +215,7 @@
             fwd_lo.start()
             feat_dn.wait_recv()
             fwd_hi.start()
+            lax.fori_loop(1, n, start_reduce, 0)
 
     filt_mate.wait_recv()
     split_filters(fx, 1)
@@ -260,12 +259,10 @@
         two = dot(gh[half], mts[...])
         sums = two[:, :pair] + two[:, pair:] + dot(gl[half], mts[:, :pair])
         a, b = halves(sums)
-        total = None
-        for r in range(NRAD):
-            here = slice(r * part_i, (r + 1) * part_i)
-            wh, wl = fh[r * pair:(r + 1) * pair, :], fl[r * pair:(r + 1) * pair, :]
-            term = dot(jnp.concatenate([a[here], b[here]], 1), jnp.concatenate([wh, wh], 0)) + dot(a[here], wl)
-            total = term if r == 0 else total + term
+        a = jnp.concatenate([a[r * part_i:(r + 1) * part_i] for r in range(NRAD)], 1)
+        b = jnp.concatenate([b[r * part_i:(r + 1) * part_i] for r in range(NRAD)], 1)
+        two = dot(jnp.concatenate([a, b], 0), fh[...])
+        total = two[:part_i] + two[part_i:] + dot(a, fl[...])
         for k in range(groups):
             ps[half, k] = total[:, k * pair:(k + 1) * pair]
         copies = []

time: 43.5 us -> 42.3 us (0.972)
  Pallas kernels: 40.9 us -> 39.7 us
    pallas_call x1, Pallas kernels: 40.9 us -> 39.7 us  [shards(): pl.pallas_call(functools.partial(kernel, n, chans), out_shape=(out, out,...]
where the time goes in v5:
time: 42.3 us; the launch traced here: 42.1 us
  Pallas kernels  39.7 us (94%)
  other arithmetic  1.76 us (4%)
  between operations  0.64 us (2%)
    pallas_call x1, Pallas kernels, shards(): pl.pallas_call(functools.partial(kernel, n, chans), out_shape=(out, out,...  39.7 us
    mul x1, other arithmetic, shards(): return (upd * live, grad * live)  1.76 us

profile of v5, /device:TPU:0, one launch (start us, length us, event | category | flops | bytes accessed | tf_op | source)
XLA Modules:
  0.0 42.1 jit_solution(14389408673639131071)
XLA Ops:
  0.6 39.7 %shard_map.86 = (f32[64,512]{1,0:T(8,128)}, f32[64,512]{1,0:T(8,128)}, f32[64,512]{1,0:T(8,128)}) custom-call(f32[64,512]{1,0:T(8,128)} %feat_in.1, f32[3,512]{1,0:T(4,128)} %pos_in.1, s32[2]{0:T(128)} %counts_in.1, s32[2,4]{1,0:T(2,128)} %nbr_in.1, s32[3,512]{1,0:T(4,128)} %wv_in.1, f32[8,64,256]{2,1,0:T(8,128)} %filt_in.1, f32[64,512]{1,0:T(8,128)} %cot_in.1), custom_call_target="tpu_custom_call" | custom-call | tf_op jit(solution)/shard_map/pallas_call | solution.py:444
  40.4 1.8 %fusion = (f32[64,512]{1,0:T(8,128)}, f32[64,512]{1,0:T(8,128)}) fusion(f32[64,512]{1,0:T(8,128)} %get-tuple-element.7, f32[64,512]{1,0:T(8,128)} %get-tuple-element.6, f32[64,512]{1,0:T(8,128)} %get-tuple-element.5), kind=kLoop, calls=%fused_computation | loop fusion | flops 65536 | bytes 655360 | tf_op jit(solution)/shard_map/mul | solution.py:453

commit v6 on v5

--- a/solution.py
+++ b/solution.py
@@ -12,6 +12,7 @@
 NB = 4
 BLK_DEV = 2
 PARTS = 2
+LOG2E = math.log2(math.e)
 MOST = 4
 SIDE = 2 * MOST + 1
 HALF = (SIDE**3 - 1) // 2
@@ -51,7 +52,7 @@
     return f, a - MOST, b - MOST, c - MOST
 
 
-def kernel(n, chans, feat_in, pos_in, counts_in, nbr_in, wv_in, filt_in, cot_in, upd, grad, live_out,
+def kernel(n, chans, feat_in, pos_in, counts_in, nbr_in, wv_in, filt_in, cot_in, upd, grad,
            feat, pos, counts, nbr, wv, filt, cot,
            f6, p6, pt, fx, fh, fl, cm, c2, gh, gl, mts, mt, vs, th, tl, ss, rb, sg, ps, rx, ug, so, sr,
            re, wo, wp, rw, rt, hb, load_s, misc_s, misc_r, red_s, red_r, gat_s, gat_r):
@@ -198,9 +199,9 @@
                 dz = own[:, 2:3] - far[2:3, :]
                 sq = jnp.minimum(dx * dx + dy * dy + dz * dz, 1.0)
                 left = 1.0 - sq
-                u = NRAD * jnp.sqrt(sq) - 0.5
-                t = jnp.exp(u)
-                g = jnp.exp(-0.5 * u * u) * (0.3 * left * left)
+                u = (sq * NRAD) * lax.rsqrt(jnp.maximum(sq, 1e-30)) - 0.5
+                t = jnp.exp2(u * LOG2E)
+                g = jnp.exp2((u * u) * (-0.5 * LOG2E)) * (0.3 * left * left)
                 for r in range(NRAD):
                     if r:
                         g = g * t
@@ -364,13 +365,12 @@
     mine, other = so[p], sr[...]
     first = jnp.where(p == 0, mine, other)
     second = jnp.where(p == 0, other, mine)
-    live_out[...] = jnp.broadcast_to(live, live_out.shape)
-    upd[...] = (fm + jnp.concatenate([first, second], 1) + far_part[:panel])
+    upd[...] = live * (fm + jnp.concatenate([first, second], 1) + far_part[:panel])
     ret_mates[1].wait_recv()
     part = cmask + far_part[panel:] + jnp.concatenate([wo[1, b] + rw[1, b] for b in range(BLK_DEV)], 1)
     ret_up.wait_recv()
     ret_dn.wait_recv()
-    grad[...] = (part + jnp.concatenate([hb[0, b] + hb[1, b] for b in range(BLK_DEV)], 1))
+    grad[...] = live * (part + jnp.concatenate([hb[0, b] + hb[1, b] for b in range(BLK_DEV)], 1))
 
     for c in (pos_up, pos_dn, feat_up, feat_dn, feat_mate, fwd_lo, fwd_hi, filt_mate, cot_mate,
               act_mate, *ret_mates.values(), ret_up, ret_dn, *sum(pre_copies, []), *sum(up_copies, [])):
@@ -382,6 +382,14 @@
         return carry
 
     lax.fori_loop(1, n, drain, 0)
+
+
+def finish(upd_in, grad_in, upd, grad, sem):
+    copies = [pltpu.make_async_copy(upd_in, upd, sem.at[0]), pltpu.make_async_copy(grad_in, grad, sem.at[1])]
+    for c in copies:
+        c.start()
+    for c in copies:
+        c.wait()
 
 
 def shards(n, chans, features, positions, counts, neighbours, wavevectors, filters, cotangent):
@@ -441,16 +449,23 @@
     whole = pl.BlockSpec(memory_space=pltpu.VMEM)
     anywhere = pl.BlockSpec(memory_space=pl.ANY)
     out = jax.ShapeDtypeStruct((panel, slots), f32)
-    upd, grad, live = pl.pallas_call(
+    results = pl.pallas_call(
         functools.partial(kernel, n, chans),
-        out_shape=(out, out, out),
+        out_shape=(out, out),
         in_specs=[anywhere] * 7,
-        out_specs=(whole, whole, whole),
+        out_specs=(whole, whole),
         scratch_shapes=scratch,
         compiler_params=pltpu.CompilerParams(
             collective_id=0, has_side_effects=True, vmem_limit_bytes=60 * 1024 * 1024),
     )(features, positions, counts, neighbours, wavevectors, filters, cotangent)
-    return upd * live, grad * live
+    return pl.pallas_call(
+        finish,
+        out_shape=(out, out),
+        in_specs=[anywhere] * 2,
+        out_specs=(anywhere, anywhere),
+        scratch_shapes=[pltpu.SemaphoreType.DMA((2,))],
+        compiler_params=pltpu.CompilerParams(vmem_limit_bytes=60 * 1024 * 1024),
+    )(*results)
 
 
 def solution(mesh):

time: 42.3 us -> 49.5 us (1.17)
  Pallas kernels: 39.7 us -> 48.8 us
  other arithmetic: 1.76 us -> 0 us
    pallas_call x1 -> x2, Pallas kernels: 39.7 us -> 48.8 us  [the longest x1 39.7 us: shards(): pl.pallas_call(functools.partial(kernel, n, chans), out_shape=(out, out),...]
    mul x1 -> x0, other arithmetic: 1.76 us -> none  [shards(): return (upd * live, grad * live)]
where the time goes in v6:
time: 49.5 us; the launch traced here: 49.4 us
  Pallas kernels  48.8 us (99%)
  between operations  0.64 us (1%)
    pallas_call x1, Pallas kernels, shards(): pl.pallas_call(functools.partial(kernel, n, chans), out_shape=(out, out),...  39.7 us
    pallas_call x1, Pallas kernels, shards(): pl.pallas_call(finish, out_shape=(out, out), in_specs=[anywhere] * 2, out...  9.06 us

profile of v6, /device:TPU:0, one launch (start us, length us, event | category | flops | bytes accessed | tf_op | source)
XLA Modules:
  0.0 49.4 jit_solution(1226197154520669957)
XLA Ops:
  0.6 39.7 %shard_map.86 = (f32[64,512]{1,0:T(8,128)}, f32[64,512]{1,0:T(8,128)}) custom-call(f32[64,512]{1,0:T(8,128)} %feat_in.1, f32[3,512]{1,0:T(4,128)} %pos_in.1, s32[2]{0:T(128)} %counts_in.1, s32[2,4]{1,0:T(2,128)} %nbr_in.1, s32[3,512]{1,0:T(4,128)} %wv_in.1, f32[8,64,256]{2,1,0:T(8,128)} %filt_in.1, f32[64,512]{1,0:T(8,128)} %cot_in.1), custom_call_target="tpu_custom_call" | custom-call | tf_op jit(solution)/shard_map/pallas_call | solution.py:452
  40.3 9.1 %shard_map.87 = (f32[64,512]{1,0:T(8,128)}, f32[64,512]{1,0:T(8,128)}) custom-call(f32[64,512]{1,0:T(8,128)} %get-tuple-element.4.upd_in, f32[64,512]{1,0:T(8,128)} %get-tuple-element.5.grad_in), custom_call_target="tpu_custom_call" | custom-call | tf_op jit(solution)/shard_map/pallas_call | solution.py:461

commit v7 on v5

--- a/solution.py
+++ b/solution.py
@@ -273,8 +273,6 @@
             copies.append(c)
         pre_copies.append(copies)
 
-    all_gather_start()
-
     cot_mate.wait_recv()
     up_copies = []
     for half in range(PARTS):
@@ -299,6 +297,8 @@
         up_copies.append(copies)
         so[0, :, here] = act[:panel]
         so[1, :, here] = act[panel:]
+        if half == 0:
+            all_gather_start()
     act_mate = remote(so.at[1 - p], sr, 9, mate)
     act_mate.start()
 

time: 42.3 us -> 41.2 us (0.974)
  Pallas kernels: 39.7 us -> 38.6 us
    pallas_call x1, Pallas kernels: 39.7 us -> 38.6 us  [shards(): pl.pallas_call(functools.partial(kernel, n, chans), out_shape=(out, out,...]
where the time goes in v7:
time: 41.2 us; the launch traced here: 41 us
  Pallas kernels  38.6 us (94%)
  other arithmetic  1.76 us (4%)
  between operations  0.64 us (2%)
    pallas_call x1, Pallas kernels, shards(): pl.pallas_call(functools.partial(kernel, n, chans), out_shape=(out, out,...  38.6 us
    mul x1, other arithmetic, shards(): return (upd * live, grad * live)  1.76 us

profile of v7, /device:TPU:0, one launch (start us, length us, event | category | flops | bytes accessed | tf_op | source)
XLA Modules:
  0.0 41.0 jit_solution(7684995100063837761)
XLA Ops:
  0.6 38.6 %shard_map.86 = (f32[64,512]{1,0:T(8,128)}, f32[64,512]{1,0:T(8,128)}, f32[64,512]{1,0:T(8,128)}) custom-call(f32[64,512]{1,0:T(8,128)} %feat_in.1, f32[3,512]{1,0:T(4,128)} %pos_in.1, s32[2]{0:T(128)} %counts_in.1, s32[2,4]{1,0:T(2,128)} %nbr_in.1, s32[3,512]{1,0:T(4,128)} %wv_in.1, f32[8,64,256]{2,1,0:T(8,128)} %filt_in.1, f32[64,512]{1,0:T(8,128)} %cot_in.1), custom_call_target="tpu_custom_call" | custom-call | tf_op jit(solution)/shard_map/pallas_call | solution.py:444
  39.2 1.8 %fusion = (f32[64,512]{1,0:T(8,128)}, f32[64,512]{1,0:T(8,128)}) fusion(f32[64,512]{1,0:T(8,128)} %get-tuple-element.7, f32[64,512]{1,0:T(8,128)} %get-tuple-element.6, f32[64,512]{1,0:T(8,128)} %get-tuple-element.5), kind=kLoop, calls=%fused_computation | loop fusion | flops 65536 | bytes 655360 | tf_op jit(solution)/shard_map/mul | solution.py:453
